TPU v7x, 32 devices: a whole 2x2x4 slice. The times are simulated.
32 devices in a mesh: dp: 8 (over y, x, core), tensor: 4 (over z).
Axes of the slice: x: 2, y: 2, z: 4, core: 2. Of those that a mesh axis runs over, the one named last changes fastest.
Arguments:
- states: float32 [4096, 2048], P('dp'), may hold values from -6 to 6
- w_query: bfloat16 [2048, 2048], P(None, 'tensor'), may hold values from -0.125 to 0.125
- w_key: bfloat16 [2048, 2048], P(None, 'tensor'), may hold values from -0.125 to 0.125
- w_value: bfloat16 [2048, 2048], P(None, 'tensor'), may hold values from -0.125 to 0.125
- w_out: bfloat16 [2048, 2048], P('tensor'), may hold values from -6 to 6
- w_gate: bfloat16 [2048, 8192], P(None, 'tensor'), may hold values from -0.125 to 0.125
- w_up: bfloat16 [2048, 8192], P(None, 'tensor'), may hold values from -0.125 to 0.125
- w_down: bfloat16 [8192, 2048], P('tensor'), may hold values from -0.0625 to 0.0625
- group_id: int32 [8], replicated, may hold values from 0 to 1, as said below
- slice_start: int32 [8], replicated, may hold values from 0 to 1152, as said below
- cont_group: int32 [8], P('dp'), may hold values from 0 to 1
- cotangent: float32 [4096, 2048], P('dp'), may hold values from -6 to 6
Outputs:
- layer_out: float32 [4096, 2048], P('dp')
- input_grad: float32 [4096, 2048], P('dp')
- grad_query: float32 [2048, 2048], P('dp', 'tensor')
- grad_key: float32 [2048, 2048], P('dp', 'tensor')
- grad_value: float32 [2048, 2048], P('dp', 'tensor')
- grad_out: float32 [2048, 2048], P('tensor', 'dp')
- grad_gate: float32 [2048, 8192], P('dp', 'tensor')
- grad_up: float32 [2048, 8192], P('dp', 'tensor')
- grad_down: float32 [8192, 2048], P('tensor', 'dp')
Inputs may be any that keep to these rules, and one draw needn't show every extreme that they name: `group_id`: exactly half of the 8 members have each group. `slice_start`: the members of one group have the starts 0, 384, 768, and so on, each once.
All inputs are finite; a program needn't handle non-finite values.
Results may differ from a plain program's by a relative error of at most 0.02.
Values may be sent and summed in bfloat16 or wider, within the bound.
A program may use at most 384 MiB of HBM per device.

v0:
```python
import jax
import jax.numpy as jnp
from jax import lax
from jax.sharding import PartitionSpec as P

HEAD = 128
PROMPT_DEV = 384


EPSILON = 1e-05
NEGATIVE = -1e30


def norm_rows(values):
    row_mean = jnp.mean(values, axis=-1, keepdims=True)
    centred = values - row_mean
    inverse = lax.rsqrt(jnp.mean(centred * centred, axis=-1, keepdims=True) + EPSILON)
    return (centred * inverse, inverse)


def norm_back(gradient, normed, inverse):
    return inverse * (
        gradient
        - jnp.mean(gradient, axis=-1, keepdims=True)
        - normed * jnp.mean(gradient * normed, axis=-1, keepdims=True)
    )


def rotary(values, positions, direction):
    full_width = values.shape[-1]
    half_width = full_width // 2
    frequency = 10000.0 ** (-jnp.arange(half_width, dtype=jnp.float32) * 2.0 / full_width)
    angles = positions.astype(jnp.float32)[:, None] * frequency[None, :]
    cosine = jnp.cos(angles)[:, None, :]
    sine_part = direction * jnp.sin(angles)[:, None, :]
    first_half = values[..., :half_width]
    second_half = values[..., half_width:]
    return jnp.concatenate(
        [
            first_half * cosine - second_half * sine_part,
            second_half * cosine + first_half * sine_part,
        ],
        axis=-1,
    )


def contract(left_side, right_side, left_dim, right_dim):
    return lax.dot_general(
        left_side,
        right_side,
        (((left_dim,), (right_dim,)), ((), ())),
        preferred_element_type=jnp.float32,
    )


def head_major(flat_rows, head_count):
    return flat_rows.reshape(flat_rows.shape[0], head_count, HEAD).transpose(1, 0, 2)


def body(
    states,
    w_query,
    w_key,
    w_value,
    w_out,
    w_gate,
    w_up,
    w_down,
    group_id,
    slice_start,
    cont_group,
    cotangent,
):
    row_count = states.shape[0]
    members = lax.axis_size("dp")
    member = lax.axis_index("dp")
    slice_rows = PROMPT_DEV
    prompt_total = members * slice_rows // 2
    local_width = w_query.shape[1]
    head_count = local_width // HEAD
    score_scale = HEAD ** (-0.5)
    row_index = jnp.arange(row_count, dtype=jnp.int32)
    is_prompt = row_index < slice_rows
    own_group = lax.dynamic_index_in_dim(group_id, member, 0, keepdims=False)
    own_start = lax.dynamic_index_in_dim(slice_start, member, 0, keepdims=False)
    positions = jnp.where(is_prompt, own_start + row_index, prompt_total + row_index - slice_rows)
    query_tag = jnp.where(is_prompt, own_group, cont_group[0])
    prompt_pos = (slice_start[:, None] + jnp.arange(slice_rows, dtype=jnp.int32)[None, :]).reshape(
        -1
    )
    prompt_tag = jnp.broadcast_to(group_id[:, None], (members, slice_rows)).reshape(-1)
    key_pos = jnp.concatenate([prompt_pos, positions[slice_rows:]])
    key_tag = jnp.concatenate(
        [prompt_tag, jnp.full((row_count - slice_rows,), 2, jnp.int32) + member]
    )
    allowed = (key_pos[None, :] <= positions[:, None]) & (
        (key_tag[None, :] == query_tag[:, None]) | (key_tag[None, :] == 2 + member)
    )
    normed_one, inverse_one = norm_rows(states)
    act_one = normed_one.astype(jnp.bfloat16)
    query_lin = jnp.dot(act_one, w_query, preferred_element_type=jnp.float32)
    key_lin = jnp.dot(act_one, w_key, preferred_element_type=jnp.float32)
    value_lin = jnp.dot(act_one, w_value, preferred_element_type=jnp.float32)
    query_rot = rotary(query_lin.reshape(row_count, head_count, HEAD), positions, 1.0).astype(
        jnp.bfloat16
    )
    key_rot = (
        rotary(key_lin.reshape(row_count, head_count, HEAD), positions, 1.0)
        .astype(jnp.bfloat16)
        .reshape(row_count, local_width)
    )
    value_low = value_lin.astype(jnp.bfloat16)
    prompt_keys, prompt_values = (
        lax.all_gather(key_rot[:slice_rows], "dp", axis=0, tiled=True),
        lax.all_gather(value_low[:slice_rows], "dp", axis=0, tiled=True),
    )
    key_heads = head_major(jnp.concatenate([prompt_keys, key_rot[slice_rows:]]), head_count)
    value_heads = head_major(jnp.concatenate([prompt_values, value_low[slice_rows:]]), head_count)
    query_heads = query_rot.transpose(1, 0, 2)

    def attend(operands):
        queries, keyset, valueset = operands
        scores = jnp.where(allowed, contract(queries, keyset, 1, 1) * score_scale, NEGATIVE)
        row_max = jnp.max(scores, axis=-1, keepdims=True)
        weights = jnp.exp(scores - row_max)
        row_total = jnp.sum(weights, axis=-1, keepdims=True)
        probabilities = (weights / row_total).astype(jnp.bfloat16)
        attended = jnp.dot(probabilities, valueset, preferred_element_type=jnp.float32)
        return (attended, (row_max + jnp.log(row_total))[:, 0])

    attended_heads, log_totals = lax.map(attend, (query_heads, key_heads, value_heads))
    mixed_low = (
        attended_heads.transpose(1, 0, 2).reshape(row_count, local_width).astype(jnp.bfloat16)
    )
    attn_branch = lax.psum(jnp.dot(mixed_low, w_out, preferred_element_type=jnp.float32), "tensor")
    resid = states + attn_branch
    normed_two, inverse_two = norm_rows(resid)
    act_two = normed_two.astype(jnp.bfloat16)
    gate_proj = jnp.dot(act_two, w_gate, preferred_element_type=jnp.float32)
    up_proj = jnp.dot(act_two, w_up, preferred_element_type=jnp.float32)
    sigmoid_gate = jax.nn.sigmoid(gate_proj)
    swish_gate = gate_proj * sigmoid_gate
    hidden = (swish_gate * up_proj).astype(jnp.bfloat16)
    ffn_branch = lax.psum(
        jnp.dot(hidden, w_down, preferred_element_type=jnp.float32).astype(jnp.bfloat16), "tensor"
    ).astype(jnp.float32)
    layer_out = resid + ffn_branch
    out_low = cotangent.astype(jnp.bfloat16)
    grad_down = contract(hidden, out_low, 0, 0)
    d_hidden = contract(out_low, w_down, 1, 1)
    d_gate = (d_hidden * up_proj * sigmoid_gate * (1.0 + gate_proj * (1.0 - sigmoid_gate))).astype(
        jnp.bfloat16
    )
    d_up = (d_hidden * swish_gate).astype(jnp.bfloat16)
    grad_gate = contract(act_two, d_gate, 0, 0)
    grad_up = contract(act_two, d_up, 0, 0)
    d_act_two = lax.psum(contract(d_gate, w_gate, 1, 1) + contract(d_up, w_up, 1, 1), "tensor")
    grad_resid = cotangent + norm_back(d_act_two, normed_two, inverse_two)
    branch_low = grad_resid.astype(jnp.bfloat16)
    grad_out = contract(mixed_low, branch_low, 0, 0)
    d_mixed = contract(branch_low, w_out, 1, 1).astype(jnp.bfloat16)
    d_mixed_heads = head_major(d_mixed, head_count)
    key_cut = members * slice_rows
    key_from = 0

    def attend_back(operands):
        queries, keyset, valueset, d_attended, log_total = operands
        scores = jnp.where(allowed, contract(queries, keyset, 1, 1) * score_scale, NEGATIVE)
        probabilities = jnp.exp(scores - log_total[:, None])
        d_probs = contract(d_attended, valueset, 1, 1)
        center = jnp.sum(probabilities * d_probs, axis=-1)
        d_scores = (probabilities * (d_probs - center[:, None])).astype(jnp.bfloat16)
        d_values = contract(probabilities.astype(jnp.bfloat16), d_attended, 0, 0)
        d_queries = jnp.dot(d_scores, keyset, preferred_element_type=jnp.float32) * score_scale
        d_keys = contract(d_scores, queries, 0, 0) * score_scale
        return (d_queries, d_keys, d_values, center)

    d_query_heads, d_key_heads, d_value_heads, centers = lax.map(
        attend_back, (query_heads, key_heads, value_heads, d_mixed_heads, log_totals)
    )
    d_key_flat = d_key_heads.transpose(1, 0, 2).reshape(-1, local_width)
    d_value_flat = d_value_heads.transpose(1, 0, 2).reshape(-1, local_width)
    d_key_prompt, d_value_prompt = (
        lax.psum_scatter(
            d_key_flat[:key_cut].astype(jnp.bfloat16), "dp", scatter_dimension=0, tiled=True
        ).astype(jnp.float32),
        lax.psum_scatter(
            d_value_flat[:key_cut].astype(jnp.bfloat16), "dp", scatter_dimension=0, tiled=True
        ).astype(jnp.float32),
    )
    d_key_rot = jnp.concatenate([d_key_prompt, d_key_flat[key_cut:]]).reshape(
        row_count, head_count, HEAD
    )
    d_value_low = jnp.concatenate([d_value_prompt, d_value_flat[key_cut:]]).astype(jnp.bfloat16)
    d_query_low = (
        rotary(d_query_heads.transpose(1, 0, 2), positions, -1.0)
        .reshape(row_count, local_width)
        .astype(jnp.bfloat16)
    )
    d_key_low = (
        rotary(d_key_rot, positions, -1.0).reshape(row_count, local_width).astype(jnp.bfloat16)
    )
    grad_query = contract(act_one, d_query_low, 0, 0)
    grad_key = contract(act_one, d_key_low, 0, 0)
    grad_value = contract(act_one, d_value_low, 0, 0)
    d_act_part = (
        contract(d_query_low, w_query, 1, 1)
        + contract(d_key_low, w_key, 1, 1)
        + contract(d_value_low, w_value, 1, 1)
    )
    d_act_one = lax.psum(d_act_part.astype(jnp.bfloat16), "tensor").astype(jnp.float32)
    input_grad = grad_resid + norm_back(d_act_one, normed_one, inverse_one)
    grad_query, grad_key, grad_value, grad_out, grad_gate, grad_up, grad_down = (
        lax.psum_scatter(
            grad_query.astype(jnp.bfloat16), "dp", scatter_dimension=0, tiled=True
        ).astype(jnp.float32),
        lax.psum_scatter(
            grad_key.astype(jnp.bfloat16), "dp", scatter_dimension=0, tiled=True
        ).astype(jnp.float32),
        lax.psum_scatter(
            grad_value.astype(jnp.bfloat16), "dp", scatter_dimension=0, tiled=True
        ).astype(jnp.float32),
        lax.psum_scatter(
            grad_out.astype(jnp.bfloat16), "dp", scatter_dimension=1, tiled=True
        ).astype(jnp.float32),
        lax.psum_scatter(
            grad_gate.astype(jnp.bfloat16), "dp", scatter_dimension=0, tiled=True
        ).astype(jnp.float32),
        lax.psum_scatter(
            grad_up.astype(jnp.bfloat16), "dp", scatter_dimension=0, tiled=True
        ).astype(jnp.float32),
        lax.psum_scatter(
            grad_down.astype(jnp.bfloat16), "dp", scatter_dimension=1, tiled=True
        ).astype(jnp.float32),
    )
    return (
        layer_out,
        input_grad,
        grad_query,
        grad_key,
        grad_value,
        grad_out,
        grad_gate,
        grad_up,
        grad_down,
    )


def solution(mesh):
    placed = (
        P("dp", None),
        P(None, "tensor"),
        P(None, "tensor"),
        P(None, "tensor"),
        P("tensor", None),
        P(None, "tensor"),
        P(None, "tensor"),
        P("tensor", None),
        P(),
        P(),
        P("dp"),
        P("dp", None),
    )
    return jax.shard_map(
        body,
        mesh=mesh,
        in_specs=placed,
        out_specs=(
            P("dp", None),
            P("dp", None),
            P("dp", "tensor"),
            P("dp", "tensor"),
            P("dp", "tensor"),
            P("tensor", "dp"),
            P("dp", "tensor"),
            P("dp", "tensor"),
            P("tensor", "dp"),
        ),
        check_vma=False,
    )
```

profile of v0, /device:TPU:0, one launch (start us, length us, event | category | flops | bytes accessed | tf_op | source)
XLA Modules:
  0.0 1272.0 jit_solution(3305001414715963454)
XLA Ops:
  9.3 2.5 reduce_sum.90
  11.8 2.9 multiply_reduce_fusion.3
  23.9 3.5 convolution_convert_fusion.9
  35.7 23.8 %all-gather.3.cloned.1.call-done = bf16[3072,512]{0,1:T(8,128)(2,1)} async-done(((bf16[384,512]{0,1:T(8,128)(2,1)}), bf16[3072,512]{0,1:T(8,128)(2,1)}) %all-gather.3.cloned.1.call-update) | async-done | bytes 3145744 | tf_op jit(solution)/shard_map/all_gather | solution.py:114
  59.5 3.2 fusion.53
  62.7 5.7 copy.39
  68.4 25.9 %all-gather.5.cloned.1.call-done = bf16[3072,512]{1,0:T(8,128)(2,1)} async-done(((bf16[384,512]{1,0:T(8,128)(2,1)}), bf16[3072,512]{1,0:T(8,128)(2,1)}) %all-gather.5.cloned.1.call-update) | async-done | bytes 3145744 | tf_op jit(solution)/shard_map/all_gather | solution.py:115
  94.3 4.1 bitcast_bitcast_fusion
  98.4 34.7 %while.30 = (s32[]{:T(128)}, bf16[4,512,128]{1,2,0:T(8,128)(2,1)S(1)}, f32[4,512]{1,0:T(4,128)}, bf16[4,512,128]{2,1,0:T(8,128)(2,1)}, bf16[4,3200,128]{2,1,0:T(...) while((s32[]{:T(128)}, ...), condition=%wide.region_5.6_spmd.clone.clone, body=%wide.region_2.5_spmd.clone.sunk.clone | while | flops 858521088 | bytes 21752440 | solution.py:131
  98.4 3.5 fusion.149
  103.0 2.7 fusion.151
  107.1 3.6 fusion.149
  111.6 2.7 fusion.151
  115.7 3.6 fusion.149
  120.3 2.7 fusion.151
  124.4 3.6 fusion.149
  129.0 2.7 fusion.151
  133.1 3.3 fusion.72
  136.5 155.1 %all-reduce.6.cloned.1.call-done = f32[512,2048]{1,0:T(8,128)} async-done(((f32[512,2048]{1,0:T(8,128)}), f32[512,2048]{1,0:T(8,128)}) %all-reduce.6.cloned.1.call-update) | async-done | bytes 4194320 | tf_op jit(solution)/shard_map/psum | solution.py:135
  291.5 4.0 fusion.68
  296.6 11.4 fusion.74
  308.1 6.2 fusion.73
  314.2 14.9 %multiply_convert_fusion.1 = (bf16[512,2048]{1,0:T(8,128)(2,1)}, bf16[512,2048]{1,0:T(8,128)(2,1)S(1)}, bf16[512,2048]{1,0:T(8,128)(2,1)}) fusion(f32[512,2048]{1,0:T(8,128)} %fusion.73, f32[512,2048]{1,0:T(8,128)} %fusion.74, bf16[2048,2048]{1,0:T(8,128)(2,1)} %param.23, f32[512,2048]{1,0:T(8,128)} %param.27), kind=kOutput, calls=%fused_computation.72 | convolution fusion | flops 4311744512 | bytes 27262976 | tf_op jit(solution)/shard_map/dot_general | solution.py:48
  329.1 7.8 fusion.75
  336.9 9.5 convolution_add_fusion
  346.5 154.1 %all-reduce.8.cloned.1.call-done = f32[512,2048]{1,0:T(8,128)} async-done(((f32[512,2048]{1,0:T(8,128)}), f32[512,2048]{1,0:T(8,128)}) %all-reduce.8.cloned.1.call-update) | async-done | bytes 4194320 | tf_op jit(solution)/shard_map/psum | solution.py:157
  500.6 4.5 fusion.67
  506.5 4.9 multiply_add_fusion
  511.4 3.5 convolution_convert_fusion.8
  515.9 73.7 %while.31 = (s32[]{:T(128)}, f32[4,512,128]{1,2,0:T(8,128)}, f32[4,3200,128]{1,2,0:T(8,128)}, bf16[4,3200,128]{1,2,0:T(8,128)(2,1)}, bf16[4,512,128]{2,1,0:T(8,1...) while((s32[]{:T(128)}, f32[4,512,128]{1,2,0:T(8,128)}, ...), condition=%wide.region_15.16_spmd.clone.clone, body=%wide.region_13.15_spmd.clone.sunk.clone | while | flops 2118925824 | bytes 63325856 | solution.py:178
  518.8 4.6 multiply_reduce_fusion.6
  524.5 2.5 fusion.163
  537.3 4.6 multiply_reduce_fusion.6
  542.9 2.5 fusion.163
  555.6 4.6 multiply_reduce_fusion.6
  561.3 2.5 fusion.163
  574.0 4.6 multiply_reduce_fusion.6
  579.7 2.5 fusion.163
  589.6 3.2 slice.132
  592.8 2.8 copy.47
  597.8 2.8 copy.49
  600.9 5.3 convolution_convert_fusion.3
  607.4 33.6 %reduce-scatter.28.cloned.1.call-done = bf16[384,512]{1,0:T(8,128)(2,1)} async-done(((bf16[3072,512]{1,0:T(8,128)(2,1)}), bf16[384,512]{1,0:T(8,128)(2,1)}) %reduce-scatter.28.cloned.1.call-update) | async-done | bytes 393232
  644.5 2.6 convolution_convert_fusion.6
  648.2 2.7 convolution_convert_fusion.5
  652.6 38.2 %reduce-scatter.30.cloned.1.call-done = bf16[384,512]{1,0:T(8,128)(2,1)} async-done(((bf16[3072,512]{1,0:T(8,128)(2,1)}), bf16[384,512]{1,0:T(8,128)(2,1)}) %reduce-scatter.30.cloned.1.call-update) | async-done | bytes 393232
  692.1 3.5 convolution_convert_fusion.4
  695.7 10.1 convolution_convert_fusion.1
  707.4 8.3 convolution_convert_fusion.2
  717.3 9.0 convolution_convert_fusion
  726.6 10.1 convolution_convert_fusion.7
  739.9 2.7 add_convert_fusion
  744.5 36.4 %reduce-scatter.14.cloned.1.call-done = bf16[256,512]{1,0:T(8,128)(2,1)} async-done(((bf16[2048,512]{1,0:T(8,128)(2,1)}), bf16[256,512]{1,0:T(8,128)(2,1)}) %reduce-scatter.14.cloned.1.call-update) | async-done | bytes 262160 | tf_op jit(solution)/shard_map/reduce_scatter | solution.py:214
  782.7 42.7 %reduce-scatter.16.cloned.1.call-done = bf16[256,512]{1,0:T(8,128)(2,1)} async-done(((bf16[2048,512]{1,0:T(8,128)(2,1)}), bf16[256,512]{1,0:T(8,128)(2,1)}) %reduce-scatter.16.cloned.1.call-update) | async-done | bytes 262160 | tf_op jit(solution)/shard_map/reduce_scatter | solution.py:217
  827.2 42.9 %reduce-scatter.18.cloned.1.call-done = bf16[256,512]{1,0:T(8,128)(2,1)} async-done(((bf16[2048,512]{1,0:T(8,128)(2,1)}), bf16[256,512]{1,0:T(8,128)(2,1)}) %reduce-scatter.18.cloned.1.call-update) | async-done | bytes 262160 | tf_op jit(solution)/shard_map/reduce_scatter | solution.py:220
  872.0 72.9 %reduce-scatter.24.cloned.1.call-done = bf16[256,2048]{1,0:T(8,128)(2,1)} async-done(((bf16[2048,2048]{1,0:T(8,128)(2,1)}), bf16[256,2048]{1,0:T(8,128)(2,1)}) %reduce-scatter.24.cloned.1.call-update) | async-done | bytes 1048592 | tf_op jit(solution)/shard_map/reduce_scatter | solution.py:229
  944.9 2.8 convert_element_type.162
  947.7 72.2 %reduce-scatter.22.cloned.1.call-done = bf16[256,2048]{1,0:T(8,128)(2,1)} async-done(((bf16[2048,2048]{1,0:T(8,128)(2,1)}), bf16[256,2048]{1,0:T(8,128)(2,1)}) %reduce-scatter.22.cloned.1.call-update) | async-done | bytes 1048592 | tf_op jit(solution)/shard_map/reduce_scatter | solution.py:226
  1020.0 2.8 convert_element_type.160
  1022.7 72.0 %reduce-scatter.26.cloned.1.call-done = bf16[2048,256]{1,0:T(8,128)(2,1)} async-done(((bf16[2048,2048]{1,0:T(8,128)(2,1)}), bf16[2048,256]{1,0:T(8,128)(2,1)}) %reduce-scatter.26.cloned.1.call-update) | async-done | bytes 1048592 | tf_op jit(solution)/shard_map/reduce_scatter | solution.py:232
  1094.7 2.7 convert_element_type.164
  1097.4 155.6 %all-reduce.10.cloned.1.call-done = (bf16[512,2048]{1,0:T(8,128)(2,1)}, bf16[512,2048]{1,0:T(8,128)(2,1)}) async-done(((bf16[512,2048]{1,0:T(8,128)(2,1)}, bf16[512,2048]{1,0:T(8,128)(2,1)}), (bf16[512,2048]{1,0:T(8,128)(2,1)}, bf16[512,2048]{1,0:T(8,128)(2,1)})) %all-reduce.10.cloned.1.call-update) | async-done | bytes 4194320 | tf_op jit(solution)/shard_map/psum | solution.py:144
  1253.0 5.9 convert_add_fusion
  1260.6 4.6 fusion.48
  (202 shorter events, 103.7 us)
Async XLA Ops:
  7.2 125.9 %copy-start = (bf16[512,2048]{1,0:T(8,128)(2,1)S(1)}, bf16[512,2048]{1,0:T(8,128)(2,1)}, u32[]{:S(2)}) copy-start(bf16[512,2048]{1,0:T(8,128)(2,1)} %param.20) | copy-start | bytes 6291460
  7.2 52.3 %all-gather.3.cloned.1.call-start = ((), (), s32[]{:S(2)}) async-start(), calls=%async_computation.9 | async-start | bytes 3538944 | tf_op jit(solution)/shard_map/all_gather | solution.py:114
  11.8 3.5 copy-start.2
  11.8 3.9 copy-start.23
  14.7 1.7 copy-start.9
  15.2 2.5 copy-start.25
  16.4 1.3 copy-start.13
  16.4 2.3 copy-start.11
  21.3 0.7 copy-start.18
  23.8 5.3 copy-start.27
  23.8 8.5 copy-start.28
  23.8 70.5 %all-gather.5.cloned.1.call-start = ((), (), s32[]{:S(2)}) async-start(), calls=%async_computation.10 | async-start | bytes 3538944 | tf_op jit(solution)/shard_map/all_gather | solution.py:115
  27.3 5.1 copy-start.21
  28.2 263.3 %all-reduce.6.cloned.1.call-start = ((), (), s32[]{:S(2)}) async-start(), calls=%async_computation.11 | async-start | bytes 8388608 | tf_op jit(solution)/shard_map/psum | solution.py:135
  62.7 31.6 %slice-start = ((bf16[512,512]{1,0:T(8,128)(2,1)}), bf16[128,512]{1,0:T(8,128)(2,1)S(1)}, s32[]{:S(2)}) async-start(bf16[512,512]{1,0:T(8,128)(2,1)} %copy-done.21), calls=%async_computation.23 | async-start | bytes 262144 | tf_op jit(solution)/shard_map/slice | solution.py:118
  133.1 3.3 copy-start.17
  136.4 364.2 %all-reduce.8.cloned.1.call-start = ((), (), s32[]{:S(2)}) async-start(), calls=%async_computation.12 | async-start | bytes 8388608 | tf_op jit(solution)/shard_map/psum | solution.py:157
  295.5 12.5 copy-start.4
  296.1 12.0 slice-start.1
  296.6 11.5 copy-start.15
  296.6 11.5 slice-start.2
  329.1 7.8 copy-start.30
  329.1 7.8 copy-start.31
  346.4 294.5 %reduce-scatter.28.cloned.1.call-start = ((), (), s32[]{:S(2)}) async-start(), calls=%async_computation.20 | async-start | bytes 3538944
  500.6 4.6 copy-start.5
  500.6 5.9 copy-start.6
  595.6 95.3 %reduce-scatter.30.cloned.1.call-start = ((), (), s32[]{:S(2)}) async-start(), calls=%async_computation.21 | async-start | bytes 3538944
  600.6 142.1 %reduce-scatter.20.cloned.1.call-start = ((), (), s32[]{:S(2)}) async-start(), calls=%async_computation.16 | async-start | bytes 2359296 | tf_op jit(solution)/shard_map/reduce_scatter | solution.py:223
  606.2 36.1 %copy-start.19 = (f32[512,64]{0,1:T(8,128)S(1)}, f32[512,64]{0,1:T(8,128)}, u32[]{:S(2)}) copy-start(f32[512,64]{0,1:T(8,128)} %copy-done.18) | copy-start | bytes 393220
  606.2 36.1 %copy-start.22 = (f32[512,64]{0,1:T(8,128)S(1)}, f32[512,64]{0,1:T(8,128)}, u32[]{:S(2)}) copy-start(f32[512,64]{0,1:T(8,128)} %get-tuple-element.297) | copy-start | bytes 393220
  606.2 38.4 %copy-start.14 = (bf16[512,2048]{1,0:T(8,128)(2,1)S(1)}, bf16[512,2048]{1,0:T(8,128)(2,1)}, u32[]{:S(2)}) copy-start(bf16[512,2048]{1,0:T(8,128)(2,1)} %copy-done.13) | copy-start | bytes 6291460
  606.2 174.7 %reduce-scatter.14.cloned.1.call-start = ((), (), s32[]{:S(2)}) async-start(), calls=%async_computation.13 | async-start | bytes 2359296 | tf_op jit(solution)/shard_map/reduce_scatter | solution.py:214
  647.2 178.2 %reduce-scatter.16.cloned.1.call-start = ((), (), s32[]{:S(2)}) async-start(), calls=%async_computation.14 | async-start | bytes 2359296 | tf_op jit(solution)/shard_map/reduce_scatter | solution.py:217
  651.0 219.2 %reduce-scatter.18.cloned.1.call-start = ((), (), s32[]{:S(2)}) async-start(), calls=%async_computation.15 | async-start | bytes 2359296 | tf_op jit(solution)/shard_map/reduce_scatter | solution.py:220
  695.6 249.3 %reduce-scatter.24.cloned.1.call-start = ((), (), s32[]{:S(2)}) async-start(), calls=%async_computation.18 | async-start | bytes 9437184 | tf_op jit(solution)/shard_map/reduce_scatter | solution.py:229
  705.7 1.6 copy-start.16
  705.8 314.2 %reduce-scatter.22.cloned.1.call-start = ((), (), s32[]{:S(2)}) async-start(), calls=%async_computation.17 | async-start | bytes 9437184 | tf_op jit(solution)/shard_map/reduce_scatter | solution.py:226
  715.7 1.6 copy-start.29
  715.7 379.0 %reduce-scatter.26.cloned.1.call-start = ((), (), s32[]{:S(2)}) async-start(), calls=%async_computation.19 | async-start | bytes 9437184 | tf_op jit(solution)/shard_map/reduce_scatter | solution.py:232
  726.3 10.4 copy-start.10
  726.3 526.7 %all-reduce.10.cloned.1.call-start = ((), (), s32[]{:S(2)}) async-start(), calls=%async_computation.22 | async-start | bytes 8388608 | tf_op jit(solution)/shard_map/psum | solution.py:144
  736.7 1.6 copy-start.12
  738.3 1.6 copy-start.8
  738.3 1.6 copy-start.20
  1253.0 5.9 copy-start.3
  1253.0 5.9 copy-start.7
  1253.0 5.9 copy-start.24
  1253.0 5.9 copy-start.26
  1260.5 4.6 copy-start.1
Sparse Core Ops, SparseCore 0:
  23.9 35.5 all-gather.2
  61.9 32.3 all-gather.4
  136.5 154.9 all-reduce.5
  346.6 153.9 all-reduce.7
  595.7 45.2 reduce-scatter.27
  644.6 46.2 reduce-scatter.29
  694.2 41.2 reduce-scatter.19
  739.6 41.2 reduce-scatter.13
  784.2 41.1 reduce-scatter.15
  828.9 41.2 reduce-scatter.17
  873.6 71.2 reduce-scatter.23
  948.6 71.2 reduce-scatter.21
  1023.4 71.2 reduce-scatter.25
  1097.7 155.3 all-reduce.9
where the time goes:
time: 1280 us; the launch traced here: 1270 us
  waiting for transfers between devices  926 us (72%)
  matrix products  199 us (16%)
  other arithmetic  74.8 us (6%)
  local copies, waits for them, and re-layouts  56.2 us (4%)
  between operations  15.3 us (1%)
    psum x1, waiting for transfers between devices, body(): lax.psum(jnp.dot(hidden, w_down, preferred_element_type=jnp.float32).asty...  156 us
    psum x1, waiting for transfers between devices, body(): lax.psum(jnp.dot(mixed_low, w_out, preferred_element_type=jnp.float32), '...  155 us
    psum x1, waiting for transfers between devices, body(): lax.psum(contract(d_gate, w_gate, 1, 1) + contract(d_up, w_up, 1, 1), 'te...  154 us
    dot_general x34, matrix products, contract(): lax.dot_general(left_side, right_side, (((left_dim,), (right_dim,)), ((),...  142 us
    reduce_scatter x1, waiting for transfers between devices, body(): lax.psum_scatter(grad_up.astype(jnp.bfloat16), 'dp', scatter_dimension=0,...  72.9 us
    reduce_scatter x1, waiting for transfers between devices, body(): lax.psum_scatter(grad_gate.astype(jnp.bfloat16), 'dp', scatter_dimension=...  72.2 us
    unnamed x16, waiting for transfers between devices  72.1 us
    reduce_scatter x1, waiting for transfers between devices, body(): lax.psum_scatter(grad_down.astype(jnp.bfloat16), 'dp', scatter_dimension=...  72 us
  transfers between devices with their start and end apart: 14, of which 13 were waited for; matrix products, arithmetic and copies ran while one was open for 8% of the time, Pallas kernels for 0%

commit v1 on v0

v1 whole, which is shorter than its diff:
```python
import functools

import jax
import jax.numpy as jnp
from jax import lax
from jax.experimental import pallas as pl
from jax.experimental.pallas import tpu as pltpu
from jax.sharding import PartitionSpec as P

HEAD = 128
PROMPT_DEV = 384
EPSILON = 1e-05
NEGATIVE = -1e30
SCALE = HEAD ** (-0.5)
LOW = jnp.bfloat16
WIDE = jnp.float32
MESH = pl.DeviceIdType.MESH
ANY = pl.BlockSpec(memory_space=pl.ANY)
VMEM = pl.BlockSpec(memory_space=pltpu.VMEM)
DMA = pltpu.SemaphoreType.DMA
VMEM_LIMIT = 60 * 2**20


def dot(left, right, left_dim=1, right_dim=0):
    return lax.dot_general(
        left, right, (((left_dim,), (right_dim,)), ((), ())), preferred_element_type=WIDE
    )


def shape(dims, dtype):
    return jax.ShapeDtypeStruct(dims, dtype)


def norm_rows(values):
    row_mean = jnp.mean(values, axis=-1, keepdims=True)
    centred = values - row_mean
    inverse = lax.rsqrt(jnp.mean(centred * centred, axis=-1, keepdims=True) + EPSILON)
    return centred * inverse, inverse


def norm_back(gradient, normed, inverse):
    return inverse * (
        gradient
        - jnp.mean(gradient, axis=-1, keepdims=True)
        - normed * jnp.mean(gradient * normed, axis=-1, keepdims=True)
    )


def rotate(values, cosine, sine):
    return values * cosine + pltpu.roll(values, HEAD // 2, 1) * sine


def flip(index, mask):
    out, bit = index, 1
    while bit <= mask:
        if mask & bit:
            out = out + bit * (1 - 2 * lax.rem(lax.div(index, bit), 2))
        bit *= 2
    return out


def bits_of(count):
    return list(range(count.bit_length() - 1))


def greet(peers):
    barrier = pltpu.get_barrier_semaphore()
    for peer in peers:
        pl.semaphore_signal(barrier, inc=1, device_id=peer, device_id_type=MESH)
    pl.semaphore_wait(barrier, len(peers))


def remote(source, target, send_sem, recv_sem, device):
    return pltpu.make_async_remote_copy(
        src_ref=source,
        dst_ref=target,
        send_sem=send_sem,
        recv_sem=recv_sem,
        device_id=device,
        device_id_type=MESH,
    )


class Line:
    scratch_count = 10

    @staticmethod
    def scratch(count, rows, width):
        return [
            pltpu.VMEM((rows, width), WIDE),
            pltpu.VMEM((count, rows, width), LOW),
            pltpu.VMEM((count, rows, width), LOW),
            pltpu.VMEM((count, rows, width), LOW),
            DMA((count,)),
            DMA((count,)),
            DMA((count,)),
            DMA((count,)),
            DMA((count,)),
            DMA((count,)),
        ]

    def __init__(self, count, refs):
        self.count = count
        (
            self.total,
            self.outgoing,
            self.from_left,
            self.from_right,
            self.out_sem,
            self.left_sem,
            self.right_sem,
            self.to_right_sem,
            self.to_left_sem,
            self.got_sem,
        ) = refs
        self.rows = self.total.shape[0]
        self.here = lax.axis_index("tensor")
        member = lax.axis_index("dp")
        self.right = (member, lax.rem(self.here + 1, count))
        self.left = (member, lax.rem(self.here + count - 1, count))

    def peers(self):
        return [self.left, self.right]

    def rightward(self, chunk):
        return remote(
            self.outgoing.at[chunk],
            self.from_left.at[chunk],
            self.out_sem.at[chunk],
            self.left_sem.at[chunk],
            self.right,
        )

    def leftward(self, chunk):
        return remote(
            self.outgoing.at[chunk],
            self.from_right.at[chunk],
            self.out_sem.at[chunk],
            self.right_sem.at[chunk],
            self.left,
        )

    def scatter_slot(self, slot, part):
        here, count = self.here, self.count

        @pl.when(here <= slot)
        def _():
            chunk = count - 1 + here - slot
            self.total[...] = part(chunk)

            @pl.when(here > 0)
            def _():
                self.rightward(chunk).wait_recv()
                self.total[...] += self.from_left[chunk].astype(WIDE)

            self.outgoing[chunk] = self.total[...].astype(LOW)
            self.rightward(chunk).start()

        @pl.when(count - 1 - here <= slot)
        def _():
            chunk = slot - (count - 1 - here)
            self.total[...] = part(chunk)

            @pl.when(here < count - 1)
            def _():
                self.leftward(chunk).wait_recv()
                self.total[...] += self.from_right[chunk].astype(WIDE)

            self.outgoing[chunk] = self.total[...].astype(LOW)
            self.leftward(chunk).start()

    def scatter_end(self, part):
        here = self.here
        self.total[...] = part(here)

        @pl.when(here > 0)
        def _():
            self.rightward(here).wait_recv()
            self.total[...] += self.from_left[here].astype(WIDE)

        @pl.when(here < self.count - 1)
        def _():
            self.leftward(here).wait_recv()
            self.total[...] += self.from_right[here].astype(WIDE)

    def piece(self, whole, chunk):
        return whole.at[pl.ds(pl.multiple_of(chunk * self.rows, self.rows), self.rows)]

    def passing(self, whole, chunk, right):
        ref = self.piece(whole, chunk)
        return remote(
            ref,
            ref,
            (self.to_right_sem if right else self.to_left_sem).at[chunk],
            self.got_sem.at[chunk],
            self.right if right else self.left,
        )

    def gather_slot(self, whole, distance):
        here, count = self.here, self.count

        @pl.when(here - distance >= 0)
        def _():
            if distance:
                self.passing(whole, here - distance, True).wait_recv()

            @pl.when(here < count - 1)
            def _():
                self.passing(whole, here - distance, True).start()

        @pl.when(here + distance <= count - 1)
        def _():
            if distance:
                self.passing(whole, here + distance, False).wait_recv()

            @pl.when(here > 0)
            def _():
                self.passing(whole, here + distance, False).start()

    def finish(self, whole):
        here, count = self.here, self.count
        for chunk in range(count):

            @pl.when(here != chunk)
            def _(chunk=chunk):
                self.rightward(chunk).wait_send()

            @pl.when((chunk <= here) & (here < count - 1))
            def _(chunk=chunk):
                self.passing(whole, chunk, True).wait_send()

            @pl.when((chunk >= here) & (here > 0))
            def _(chunk=chunk):
                self.passing(whole, chunk, False).wait_send()


class Halving:
    def __init__(self, pairs, order, send, recv, send_sem, recv_sem):
        self.pairs, self.order = pairs, order
        self.send, self.recv = send, recv
        self.send_sem, self.recv_sem = send_sem, recv_sem
        self.member = lax.axis_index("dp")
        self.tensor = lax.axis_index("tensor")
        self.high = lax.div(self.member, 2)

    def stage(self, mask):
        for position, bit in enumerate(self.order):
            if mask >> bit & 1:
                return position
        return len(self.order)

    def sends(self):
        masks = range(1, self.pairs)
        return sorted(masks, key=lambda mask: (self.stage(mask), -mask.bit_count()))

    def copy(self, mask):
        bit = 1 << self.order[self.stage(mask)]
        return remote(
            self.send.at[mask - 1],
            self.recv.at[mask - 1],
            self.send_sem.at[mask - 1],
            self.recv_sem.at[mask - 1],
            (flip(self.member, bit * 2), self.tensor),
        )

    def arrived(self, mask):
        slots = [mask | 1 << bit for bit in self.order[: self.stage(mask)]]
        for slot in slots:
            self.copy(slot).wait_recv()
        return [slot - 1 for slot in slots]

    def target(self, mask):
        return flip(self.high, mask)

    def push(self, mask, own):
        slots = self.arrived(mask)
        own(self.target(mask), slots, self.recv, self.send.at[mask - 1])
        self.copy(mask).start()

    def end(self, own, out):
        own(self.target(0), self.arrived(0), self.recv, out)

    def finish(self):
        for mask in range(1, self.pairs):
            self.copy(mask).wait_send()


class Weight:
    @staticmethod
    def scratch(pairs, rows, block, width, parts):
        return [
            pltpu.VMEM((pairs, 2 * rows, block), LOW),
            pltpu.VMEM((2 * rows, width), LOW),
            pltpu.VMEM((pairs - 1, block, width), LOW),
            pltpu.VMEM((pairs - 1, block, width), LOW),
            DMA((pairs - 1,)),
            DMA((pairs - 1,)),
            DMA((pairs + parts,)),
            DMA((pairs + parts,)),
            DMA((pairs + parts,)),
        ]

    scratch_count = 9

    def __init__(self, pairs, order, left, rights, refs):
        (
            self.lhs,
            self.rhs,
            send,
            recv,
            send_sem,
            recv_sem,
            self.local_sem,
            self.core_send,
            self.core_recv,
        ) = refs
        self.left, self.rights = left, rights
        self.pairs = pairs
        self.rows = self.lhs.shape[1] // 2
        self.block = self.lhs.shape[2]
        self.width = self.rhs.shape[1]
        self.halving = Halving(pairs, order, send, recv, send_sem, recv_sem)
        member = self.halving.member
        self.parity = lax.rem(member, 2)
        self.partner = (flip(member, 1), self.halving.tensor)

    def copies(self):
        out = []
        rows, block = self.rows, self.block

        def columns_of(index):
            if len(self.left.shape) == 3:
                return self.left.at[index]
            return self.left.at[:, pl.ds(pl.multiple_of(index * block, block), block)]

        for pair in range(self.pairs):
            out.append(
                (
                    columns_of(2 * pair + self.parity),
                    self.lhs.at[pair, pl.ds(0, rows)],
                    columns_of(2 * pair + 1 - self.parity),
                    self.lhs.at[pair, pl.ds(rows, rows)],
                )
            )
        at = 0
        for right in self.rights:
            columns = pl.ds(at, right.shape[1])
            at += right.shape[1]
            out.append(
                (
                    right,
                    self.rhs.at[pl.ds(0, rows), columns],
                    right,
                    self.rhs.at[pl.ds(rows, rows), columns],
                )
            )
        local = [
            pltpu.make_async_copy(a, b, self.local_sem.at[i]) for i, (a, b, _, _) in enumerate(out)
        ]
        across = [
            remote(a, b, self.core_send.at[i], self.core_recv.at[i], self.partner)
            for i, (_, _, a, b) in enumerate(out)
        ]
        return local, across

    def start(self):
        local, across = self.copies()
        for copy in across + local:
            copy.start()

    def ready(self):
        local, across = self.copies()
        for copy in local:
            copy.wait()
        for copy in across:
            copy.wait_recv()

    def own(self, target, slots, recv, out):
        tile = 512
        for start in range(0, self.width, tile):
            columns = pl.ds(start, tile)
            total = dot(self.lhs[target], self.rhs[:, columns], 0, 0)
            for slot in slots:
                total += recv[slot, :, columns].astype(WIDE)
            out[:, columns] = total.astype(LOW)

    def push(self, mask):
        self.halving.push(mask, self.own)

    def end(self, out):
        self.halving.end(self.own, out)

    def finish(self):
        self.halving.finish()
        for copy in self.copies()[1]:
            copy.wait_send()


def in_blocks(left, members):
    block = left.shape[1] // members
    if block % 128 == 0:
        return left
    return left.reshape(left.shape[0], members, block).transpose(1, 0, 2)


def member_peers(members):
    member, tensor = lax.axis_index("dp"), lax.axis_index("tensor")
    return [(flip(member, 1 << bit), tensor) for bit in bits_of(members)]


def project_kernel(
    members,
    states,
    w_query,
    w_key,
    w_value,
    cosine,
    sine,
    cotangent,
    act,
    query,
    key,
    value,
    out_low,
    keys_all,
    values_all,
    send_sem,
    recv_sem,
    local_sem,
):
    member, tensor = lax.axis_index("dp"), lax.axis_index("tensor")
    width = query.shape[1]
    greet(member_peers(members))
    rows = 64
    for start in range(0, states.shape[0], rows):
        span = pl.ds(start, rows)
        act[span] = norm_rows(states[span])[0].astype(LOW)

    def turned(weight, out):
        linear = dot(act[...], weight[...])
        for start in range(0, width, HEAD):
            out[:, start : start + HEAD] = rotate(
                linear[:, start : start + HEAD], cosine[...], sine[...]
            ).astype(LOW)

    high = [bit for bit in bits_of(members) if bit]
    orders = (high + [0], high[::-1] + [0])
    owns, alls = (key, value), (keys_all, values_all)

    def copy(flow, mask, bit):
        slot = mask | 1 << bit
        place = alls[flow].at[flip(member, mask)]
        return remote(
            place if mask else owns[flow].at[pl.ds(0, PROMPT_DEV)],
            place,
            send_sem.at[flow, slot],
            recv_sem.at[flow, slot],
            (flip(member, 1 << bit), tensor),
        )

    def forward(flow, mask):
        order = orders[flow]
        last = max([order.index(bit) for bit in order if mask >> bit & 1], default=-1)
        for bit in order[last + 1 :]:
            copy(flow, mask, bit).start()

    def came_by(flow, mask):
        order = orders[flow]
        bit = order[max(order.index(bit) for bit in order if mask >> bit & 1)]
        return copy(flow, mask ^ 1 << bit, bit)

    def keep(flow):
        return pltpu.make_async_copy(
            owns[flow].at[pl.ds(0, PROMPT_DEV)], alls[flow].at[member], local_sem.at[flow]
        )

    turned(w_key, key)
    forward(0, 0)
    value[...] = dot(act[...], w_value[...]).astype(LOW)
    forward(1, 0)
    keep(0).start()
    keep(1).start()
    turned(w_query, query)
    for start in range(0, states.shape[0], rows):
        span = pl.ds(start, rows)
        out_low[span] = cotangent[span].astype(LOW)
    masks = range(1, members)
    inner = sorted([mask for mask in masks if not mask & 1], key=lambda mask: mask.bit_count())
    for mask in inner:
        for flow in (0, 1):
            turn = flow if not mask & 2 else flow
            came_by(turn, mask).wait_recv()
            forward(turn, mask)
    for mask in masks:
        if mask & 1:
            for flow in (0, 1):
                came_by(flow, mask).wait_recv()
    for flow in (0, 1):
        keep(flow).wait()
        for mask in masks:
            came_by(flow, mask).wait_send()


def project(members, states, w_query, w_key, w_value, cosine, sine, cotangent):
    rows, depth = states.shape
    width = w_query.shape[1]
    return pl.pallas_call(
        functools.partial(project_kernel, members),
        out_shape=[
            shape((rows, depth), LOW),
            shape((rows, width), LOW),
            shape((rows, width), LOW),
            shape((rows, width), LOW),
            shape((rows, depth), LOW),
            shape((members, PROMPT_DEV, width), LOW),
            shape((members, PROMPT_DEV, width), LOW),
        ],
        in_specs=[VMEM] * 7,
        out_specs=[VMEM] * 5 + [ANY] * 2,
        scratch_shapes=[DMA((2, members)), DMA((2, members)), DMA((2,))],
        compiler_params=pltpu.CompilerParams(
            collective_id=1, has_side_effects=True, vmem_limit_bytes=VMEM_LIMIT
        ),
        name="project",
    )(states, w_query, w_key, w_value, cosine, sine, cotangent)


def attend_kernel(
    half, plan, query, key, value, keys_all, values_all, mixed, attended, log_total
):
    def part(start, count, steps, offset):
        span = pl.ds(start, count)
        queries = query[span]
        allowed = lax.broadcasted_iota(jnp.int32, (count, count), 0) >= lax.broadcasted_iota(
            jnp.int32, (count, count), 1
        )
        scores = jnp.where(allowed, dot(queries, key[span], 1, 1) * SCALE, NEGATIVE)
        top = jnp.max(scores, axis=-1, keepdims=True)
        weights = jnp.exp(scores - top)
        total = jnp.sum(weights, axis=-1, keepdims=True)
        result = dot(weights.astype(LOW), value[span])

        def step(index, carry):
            top, total, result = carry
            place = plan[offset + index]
            scores = dot(queries, keys_all[place], 1, 1) * SCALE
            higher = jnp.maximum(top, jnp.max(scores, axis=-1, keepdims=True))
            fade = jnp.exp(top - higher)
            weights = jnp.exp(scores - higher)
            total = total * fade + jnp.sum(weights, axis=-1, keepdims=True)
            result = result * fade + dot(weights.astype(LOW), values_all[place])
            return higher, total, result

        top, total, result = lax.fori_loop(0, steps, step, (top, total, result))
        result = result / total
        mixed[span] = result.astype(LOW)
        attended[span] = result
        log_total[span] = jnp.broadcast_to(top + jnp.log(total), (count, HEAD))

    part(0, PROMPT_DEV, plan[0], 1)
    part(PROMPT_DEV, query.shape[0] - PROMPT_DEV, half, 1 + half)


def attend(plan, query, key, value, keys_all, values_all):
    rows, width = query.shape
    members = keys_all.shape[0]
    head = pl.BlockSpec((rows, HEAD), lambda h, _: (0, h))
    every = pl.BlockSpec((members, PROMPT_DEV, HEAD), lambda h, _: (0, 0, h))
    return pl.pallas_call(
        functools.partial(attend_kernel, members // 2),
        out_shape=[
            shape((rows, width), LOW),
            shape((rows, width), WIDE),
            shape((rows, width), WIDE),
        ],
        grid_spec=pltpu.PrefetchScalarGridSpec(
            num_scalar_prefetch=1,
            grid=(width // HEAD,),
            in_specs=[head, head, head, every, every],
            out_specs=[head, head, head],
        ),
        compiler_params=pltpu.CompilerParams(vmem_limit_bytes=VMEM_LIMIT),
        name="attend",
    )(plan, query, key, value, keys_all, values_all)


def attend_back_kernel(
    half,
    plan,
    query,
    key,
    value,
    keys_all,
    values_all,
    branch_low,
    w_out,
    attended,
    log_total,
    cosine,
    sine,
    d_query,
    d_keys_all,
    d_values_all,
    d_key_own,
    d_value_own,
    d_mixed,
    key_total,
    value_total,
):
    d_mixed[...] = dot(branch_low[...], w_out[...], 1, 1).astype(LOW)
    key_total[...] = jnp.zeros_like(key_total)
    value_total[...] = jnp.zeros_like(value_total)

    def part(start, count, steps, offset):
        span = pl.ds(start, count)
        queries, d_attended = query[span], d_mixed[span]
        log_sum = log_total[span][:, :1]
        center = jnp.sum(d_attended.astype(WIDE) * attended[span], axis=-1, keepdims=True)

        def back(scores, keys, values):
            probabilities = jnp.exp(scores - log_sum)
            d_scores = (probabilities * (dot(d_attended, values, 1, 1) - center)).astype(LOW)
            return (
                dot(d_scores, keys),
                dot(d_scores, queries, 0, 0),
                dot(probabilities.astype(LOW), d_attended, 0, 0),
            )

        allowed = lax.broadcasted_iota(jnp.int32, (count, count), 0) >= lax.broadcasted_iota(
            jnp.int32, (count, count), 1
        )
        scores = jnp.where(allowed, dot(queries, key[span], 1, 1) * SCALE, NEGATIVE)
        d_queries, d_own_keys, d_own_values = back(scores, key[span], value[span])

        def step(index, d_queries):
            place = plan[offset + index]
            keys, values = keys_all[place], values_all[place]
            more, d_keys, d_values = back(dot(queries, keys, 1, 1) * SCALE, keys, values)
            key_total[place] += d_keys
            value_total[place] += d_values
            return d_queries + more

        d_queries = lax.fori_loop(0, steps, step, d_queries) * SCALE
        d_query[span] = rotate(d_queries, cosine[span], -sine[span]).astype(LOW)
        return d_own_keys, d_own_values

    member = plan[1 + 2 * half]
    d_own_keys, d_own_values = part(0, PROMPT_DEV, plan[0], 1)
    key_total[member] += d_own_keys
    value_total[member] += d_own_values
    d_own_keys, d_own_values = part(PROMPT_DEV, query.shape[0] - PROMPT_DEV, half, 1 + half)
    late = pl.ds(PROMPT_DEV, query.shape[0] - PROMPT_DEV)
    d_key_own[...] = rotate(d_own_keys * SCALE, cosine[late], -sine[late]).astype(LOW)
    d_value_own[...] = d_own_values.astype(LOW)
    d_keys_all[...] = (key_total[...] * SCALE).astype(LOW)
    d_values_all[...] = value_total[...].astype(LOW)


def attend_back(
    plan, query, key, value, keys_all, values_all, branch_low, w_out, attended, log_total, cosine, sine
):
    rows, width = query.shape
    members = keys_all.shape[0]
    depth = branch_low.shape[1]
    late = rows - PROMPT_DEV
    head = pl.BlockSpec((rows, HEAD), lambda h, _: (0, h))
    every = pl.BlockSpec((members, PROMPT_DEV, HEAD), lambda h, _: (0, 0, h))
    own = pl.BlockSpec((late, HEAD), lambda h, _: (0, h))
    table = pl.BlockSpec((rows, HEAD), lambda h, _: (0, 0))
    return pl.pallas_call(
        functools.partial(attend_back_kernel, members // 2),
        out_shape=[
            shape((rows, width), LOW),
            shape((members, PROMPT_DEV, width), LOW),
            shape((members, PROMPT_DEV, width), LOW),
            shape((late, width), LOW),
            shape((late, width), LOW),
        ],
        grid_spec=pltpu.PrefetchScalarGridSpec(
            num_scalar_prefetch=1,
            grid=(width // HEAD,),
            in_specs=[
                head,
                head,
                head,
                every,
                every,
                pl.BlockSpec((rows, depth), lambda h, _: (0, 0)),
                pl.BlockSpec((HEAD, depth), lambda h, _: (h, 0)),
                head,
                head,
                table,
                table,
            ],
            out_specs=[head, every, every, own, own],
            scratch_shapes=[
                pltpu.VMEM((rows, HEAD), LOW),
                pltpu.VMEM((members, PROMPT_DEV, HEAD), WIDE),
                pltpu.VMEM((members, PROMPT_DEV, HEAD), WIDE),
            ],
        ),
        compiler_params=pltpu.CompilerParams(vmem_limit_bytes=VMEM_LIMIT),
        name="attend_back",
    )(
        plan, query, key, value, keys_all, values_all, branch_low, w_out, attended, log_total, cosine, sine
    )


def branch_kernel(count, mixed, w_out, states, act, resid, state_sem, *line_refs):
    line = Line(count, line_refs)
    rows = line.rows
    chunk_rows = pl.ds(pl.multiple_of(line.here * rows, rows), rows)
    fetch = pltpu.make_async_copy(states.at[chunk_rows], resid, state_sem)
    fetch.start()
    greet(line.peers())

    def part(chunk):
        return dot(mixed[pl.ds(pl.multiple_of(chunk * rows, rows), rows)], w_out[...])

    for slot in range(count - 1):
        line.scatter_slot(slot, part)
    line.scatter_end(part)
    fetch.wait()
    resid[...] += line.total[...]
    act[chunk_rows] = norm_rows(resid[...])[0].astype(LOW)
    for distance in range(count):
        line.gather_slot(act, distance)
    line.finish(act)


def branch(count, mixed, w_out, states):
    rows, depth = states.shape
    return pl.pallas_call(
        functools.partial(branch_kernel, count),
        out_shape=[shape((rows, depth), LOW), shape((rows // count, depth), WIDE)],
        in_specs=[VMEM, VMEM, ANY],
        out_specs=[VMEM, VMEM],
        scratch_shapes=[DMA] + Line.scratch(count, rows // count, depth),
        compiler_params=pltpu.CompilerParams(
            collective_id=2, has_side_effects=True, vmem_limit_bytes=VMEM_LIMIT
        ),
        name="branch",
    )(mixed, w_out, states)


def feed_kernel(
    act, out_low, w_gate, w_up, w_down, ffn, d_act, hidden, d_gate, d_up, ffn_total, d_total
):
    step = pl.program_id(0)
    gate = dot(act[...], w_gate[...])
    up = dot(act[...], w_up[...])
    d_hidden = dot(out_low[...], w_down[...], 1, 1)
    sigmoid = jax.nn.sigmoid(gate)
    swish = gate * sigmoid
    hidden[...] = (swish * up).astype(LOW)
    d_gate[...] = (d_hidden * up * sigmoid * (1.0 + gate * (1.0 - sigmoid))).astype(LOW)
    d_up[...] = (d_hidden * swish).astype(LOW)
    more = dot(hidden[...], w_down[...])
    d_more = dot(d_gate[...], w_gate[...], 1, 1) + dot(d_up[...], w_up[...], 1, 1)

    @pl.when(step == 0)
    def _():
        ffn_total[...] = more
        d_total[...] = d_more

    @pl.when(step > 0)
    def _():
        ffn_total[...] += more
        d_total[...] += d_more

    @pl.when(step == pl.num_programs(0) - 1)
    def _():
        ffn[...] = ffn_total[...].astype(LOW)
        d_act[...] = d_total[...].astype(LOW)


def feed(act, out_low, w_gate, w_up, w_down):
    rows, depth = act.shape
    units = w_gate.shape[1]
    tile = 512
    whole = pl.BlockSpec((rows, depth), lambda i: (0, 0))
    across = pl.BlockSpec((depth, tile), lambda i: (0, i))
    down = pl.BlockSpec((tile, depth), lambda i: (i, 0))
    inner = pl.BlockSpec((rows, tile), lambda i: (0, i))
    return pl.pallas_call(
        feed_kernel,
        out_shape=[shape((rows, depth), LOW)] * 2 + [shape((rows, units), LOW)] * 3,
        grid=(units // tile,),
        in_specs=[whole, whole, across, across, down],
        out_specs=[whole, whole, inner, inner, inner],
        scratch_shapes=[pltpu.VMEM((rows, depth), WIDE)] * 2,
        compiler_params=pltpu.CompilerParams(vmem_limit_bytes=VMEM_LIMIT),
        name="feed",
    )(act, out_low, w_gate, w_up, w_down)


def second_kernel(
    count,
    pairs,
    d_act,
    resid,
    cotangent,
    act,
    d_gate,
    d_up,
    branch_low,
    grad_resid,
    grad_gate,
    grad_up,
    cot_sem,
    *refs,
):
    line = Line(count, refs[: Line.scratch_count])
    refs = refs[Line.scratch_count :]
    order = bits_of(pairs)
    flows = [
        Weight(pairs, order, act, [d_gate], refs[: Weight.scratch_count]),
        Weight(pairs, order[::-1], act, [d_up], refs[Weight.scratch_count :]),
    ]
    rows = line.rows
    chunk_rows = pl.ds(pl.multiple_of(line.here * rows, rows), rows)
    fetch = pltpu.make_async_copy(cotangent.at[chunk_rows], grad_resid, cot_sem)
    fetch.start()
    greet(line.peers() + member_peers(2 * pairs))

    def part(chunk):
        return d_act[pl.ds(pl.multiple_of(chunk * rows, rows), rows)].astype(WIDE)

    for flow in flows:
        flow.start()
    line.scatter_slot(0, part)
    for flow in flows:
        flow.ready()
        flow.push(flow.halving.sends()[0])
    sends = max(1, len(flows[0].halving.sends()))
    first = [mask for mask in flows[0].halving.sends() if flows[0].halving.stage(mask) == 0]
    for index in range(1, len(first)):
        for flow in flows:
            flow.push(flow.halving.sends()[index])
    for slot in range(1, count - 1):
        line.scatter_slot(slot, part)
    line.scatter_end(part)
    fetch.wait()
    normed, inverse = norm_rows(resid[...])
    grad_resid[...] += norm_back(line.total[...], normed, inverse)
    branch_low[chunk_rows] = grad_resid[...].astype(LOW)
    line.gather_slot(branch_low, 0)
    for index in range(len(first), sends):
        for flow in flows:
            flow.push(flow.halving.sends()[index])
    for distance in range(1, count):
        line.gather_slot(branch_low, distance)
    flows[0].end(grad_gate)
    flows[1].end(grad_up)
    for flow in flows:
        flow.finish()
    line.finish(branch_low)


def second(count, members, d_act, resid, cotangent, act, d_gate, d_up):
    rows, depth = cotangent.shape
    units = d_gate.shape[1]
    pairs = members // 2
    block = depth // members
    return pl.pallas_call(
        functools.partial(second_kernel, count, pairs),
        out_shape=[
            shape((rows, depth), LOW),
            shape((rows // count, depth), WIDE),
            shape((block, units), LOW),
            shape((block, units), LOW),
        ],
        in_specs=[VMEM, VMEM, ANY, ANY, ANY, ANY],
        out_specs=[VMEM] * 4,
        scratch_shapes=[DMA]
        + Line.scratch(count, rows // count, depth)
        + Weight.scratch(pairs, rows, block, units, 1)
        + Weight.scratch(pairs, rows, block, units, 1),
        compiler_params=pltpu.CompilerParams(
            collective_id=3, has_side_effects=True, vmem_limit_bytes=VMEM_LIMIT
        ),
        name="second",
    )(d_act, resid, cotangent, in_blocks(act, members), d_gate, d_up)


def owner_kernel(
    pairs,
    d_keys_all,
    d_values_all,
    d_key_own,
    d_value_own,
    cosine,
    sine,
    d_key,
    d_value,
    *refs,
):
    member, tensor = lax.axis_index("dp"), lax.axis_index("tensor")
    parity = lax.rem(member, 2)
    partner = (flip(member, 1), tensor)
    order = bits_of(pairs)
    width = d_key.shape[1]
    flows = []
    for index, source in enumerate((d_keys_all, d_values_all)):
        mine, theirs, send, recv, send_sem, recv_sem, local_sem, core_send, core_recv = refs[
            9 * index : 9 * index + 9
        ]
        halving = Halving(pairs, order[::-1] if index else order, send, recv, send_sem, recv_sem)
        local = [
            pltpu.make_async_copy(source.at[2 * pair + parity], mine.at[pair], local_sem.at[pair])
            for pair in range(pairs)
        ]
        across = [
            remote(
                source.at[2 * pair + 1 - parity],
                theirs.at[pair],
                core_send.at[pair],
                core_recv.at[pair],
                partner,
            )
            for pair in range(pairs)
        ]

        def own(target, slots, recv, out, mine=mine, theirs=theirs):
            total = mine[target].astype(WIDE) + theirs[target].astype(WIDE)
            for slot in slots:
                total += recv[slot].astype(WIDE)
            out[...] = total.astype(out.dtype)

        flows.append((halving, local, across, own))
    greet(member_peers(2 * pairs))
    for _, local, across, _ in flows:
        for copy in across + local:
            copy.start()
    for halving, local, across, own in flows:
        for copy in local:
            copy.wait()
        for copy in across:
            copy.wait_recv()
        halving.push(halving.sends()[0], own)
    late = pl.ds(PROMPT_DEV, d_key.shape[0] - PROMPT_DEV)
    d_key[late] = d_key_own[...]
    d_value[late] = d_value_own[...]
    for index in range(1, pairs - 1):
        for halving, _, _, own in flows:
            halving.push(halving.sends()[index], own)
    early = pl.ds(0, PROMPT_DEV)
    total = refs[18]
    flows[0][0].end(flows[0][3], total)
    for start in range(0, width, HEAD):
        d_key[early, start : start + HEAD] = rotate(
            total[:, start : start + HEAD], cosine[early], -sine[early]
        ).astype(LOW)
    flows[1][0].end(flows[1][3], d_value.at[early])
    for halving, _, across, _ in flows:
        halving.finish()
        for copy in across:
            copy.wait_send()


def owner(members, d_keys_all, d_values_all, d_key_own, d_value_own, cosine, sine):
    width = d_key_own.shape[1]
    rows = cosine.shape[0]
    pairs = members // 2
    flow = [
        pltpu.VMEM((pairs, PROMPT_DEV, width), LOW),
        pltpu.VMEM((pairs, PROMPT_DEV, width), LOW),
        pltpu.VMEM((pairs - 1, PROMPT_DEV, width), LOW),
        pltpu.VMEM((pairs - 1, PROMPT_DEV, width), LOW),
        DMA((pairs - 1,)),
        DMA((pairs - 1,)),
        DMA((pairs,)),
        DMA((pairs,)),
        DMA((pairs,)),
    ]
    return pl.pallas_call(
        functools.partial(owner_kernel, pairs),
        out_shape=[shape((rows, width), LOW)] * 2,
        in_specs=[ANY, ANY] + [VMEM] * 4,
        out_specs=[VMEM] * 2,
        scratch_shapes=flow + flow + [pltpu.VMEM((PROMPT_DEV, width), WIDE)],
        compiler_params=pltpu.CompilerParams(
            collective_id=4, has_side_effects=True, vmem_limit_bytes=VMEM_LIMIT
        ),
        name="owner",
    )(d_keys_all, d_values_all, d_key_own, d_value_own, cosine, sine)


def first_kernel(
    count,
    pairs,
    d_query,
    d_key,
    d_value,
    w_query,
    w_key,
    w_value,
    grad_resid,
    states,
    act,
    mixed,
    branch_low,
    hidden,
    out_low,
    far_query,
    far_key,
    far_value,
    input_grad,
    grad_down,
    grad_out,
    grad_inner,
    state,
    state_sem,
    *refs,
):
    line = Line(count, refs[: Line.scratch_count])
    refs = refs[Line.scratch_count :]
    step = Weight.scratch_count
    order = bits_of(pairs)
    flows = [
        Weight(pairs, order, out_low, [hidden], refs[:step]),
        Weight(pairs, order[::-1], branch_low, [mixed], refs[step : 2 * step]),
        Weight(pairs, order[::-1], act, [far_query, far_key, far_value], refs[2 * step :]),
    ]
    rows = line.rows
    chunk_rows = pl.ds(pl.multiple_of(line.here * rows, rows), rows)
    fetch = pltpu.make_async_copy(states.at[chunk_rows], state, state_sem)
    fetch.start()
    greet(line.peers() + member_peers(2 * pairs))

    def part(chunk):
        span = pl.ds(pl.multiple_of(chunk * rows, rows), rows)
        return (
            dot(d_query[span], w_query[...], 1, 1)
            + dot(d_key[span], w_key[...], 1, 1)
            + dot(d_value[span], w_value[...], 1, 1)
        )

    for flow in flows:
        flow.start()
    line.scatter_slot(0, part)
    for flow in flows:
        flow.ready()
        flow.push(flow.halving.sends()[0])
    sends = len(flows[0].halving.sends())
    early = [mask for mask in flows[0].halving.sends() if flows[0].halving.stage(mask) == 0]
    for index in range(1, len(early)):
        for flow in flows:
            flow.push(flow.halving.sends()[index])
    for slot in range(1, count - 1):
        line.scatter_slot(slot, part)
    line.scatter_end(part)
    fetch.wait()
    normed, inverse = norm_rows(state[...])
    input_grad[chunk_rows] = (
        grad_resid[...] + norm_back(line.total[...], normed, inverse)
    ).astype(LOW)
    line.gather_slot(input_grad, 0)
    for index in range(len(early), sends):
        for flow in flows:
            flow.push(flow.halving.sends()[index])
    for distance in range(1, count):
        line.gather_slot(input_grad, distance)
    for flow, out in zip(flows, (grad_down, grad_out, grad_inner)):
        flow.end(out)
    for flow in flows:
        flow.finish()
    line.finish(input_grad)


def first(
    count,
    members,
    d_query,
    d_key,
    d_value,
    w_query,
    w_key,
    w_value,
    grad_resid,
    states,
    act,
    mixed,
    branch_low,
    hidden,
    out_low,
):
    rows, depth = states.shape
    width, units = d_query.shape[1], hidden.shape[1]
    pairs = members // 2
    block = depth // members
    return pl.pallas_call(
        functools.partial(first_kernel, count, pairs),
        out_shape=[
            shape((rows, depth), LOW),
            shape((block, units), LOW),
            shape((block, width), LOW),
            shape((block, 3 * width), LOW),
        ],
        in_specs=[VMEM] * 7 + [ANY] * 9,
        out_specs=[VMEM] * 4,
        scratch_shapes=[pltpu.VMEM((rows // count, depth), WIDE), DMA]
        + Line.scratch(count, rows // count, depth)
        + Weight.scratch(pairs, rows, block, units, 1)
        + Weight.scratch(pairs, rows, block, width, 1)
        + Weight.scratch(pairs, rows, block, 3 * width, 3),
        compiler_params=pltpu.CompilerParams(
            collective_id=5, has_side_effects=True, vmem_limit_bytes=VMEM_LIMIT
        ),
        name="first",
    )(
        d_query,
        d_key,
        d_value,
        w_query,
        w_key,
        w_value,
        grad_resid,
        states,
        in_blocks(act, members),
        mixed,
        in_blocks(branch_low, members),
        hidden,
        in_blocks(out_low, members),
        d_query,
        d_key,
        d_value,
    )


def body(
    states,
    w_query,
    w_key,
    w_value,
    w_out,
    w_gate,
    w_up,
    w_down,
    group_id,
    slice_start,
    cont_group,
    cotangent,
):
    rows = states.shape[0]
    members = lax.axis_size("dp")
    count = lax.axis_size("tensor")
    member = lax.axis_index("dp")
    half = members // 2
    index = jnp.arange(rows, dtype=jnp.int32)
    own_group = lax.dynamic_index_in_dim(group_id, member, 0, keepdims=False)
    own_start = lax.dynamic_index_in_dim(slice_start, member, 0, keepdims=False)
    positions = jnp.where(
        index < PROMPT_DEV, own_start + index, half * PROMPT_DEV + index - PROMPT_DEV
    )
    frequency = 10000.0 ** (-jnp.arange(HEAD // 2, dtype=WIDE) * 2.0 / HEAD)
    angles = positions.astype(WIDE)[:, None] * frequency[None, :]
    cosine = jnp.concatenate([jnp.cos(angles)] * 2, axis=1)
    sine = jnp.sin(angles)
    sine = jnp.concatenate([-sine, sine], axis=1)
    everyone = jnp.arange(members, dtype=jnp.int32)
    starts = jnp.arange(half, dtype=jnp.int32) * PROMPT_DEV

    def in_order(group):
        found = (group_id[None, :] == group) & (slice_start[None, :] == starts[:, None])
        return jnp.sum(jnp.where(found, everyone[None, :], 0), axis=1)

    plan = jnp.concatenate(
        [
            (own_start // PROMPT_DEV)[None],
            in_order(own_group),
            in_order(cont_group[0]),
            member[None],
        ]
    ).astype(jnp.int32)

    act_one, query, key, value, out_low, keys_all, values_all = project(
        members, states, w_query, w_key, w_value, cosine, sine, cotangent
    )
    mixed, attended, log_total = attend(plan, query, key, value, keys_all, values_all)
    act_two, resid = branch(count, mixed, w_out, states)
    ffn, d_act_two, hidden, d_gate, d_up = feed(act_two, out_low, w_gate, w_up, w_down)
    branch_low, grad_resid, grad_gate, grad_up = second(
        count, members, d_act_two, resid, cotangent, act_two, d_gate, d_up
    )
    ffn, branch_low = lax.optimization_barrier((ffn, branch_low))
    ffn = lax.psum_scatter(ffn, "tensor", scatter_dimension=0, tiled=True)
    d_query, d_keys_all, d_values_all, d_key_own, d_value_own = attend_back(
        plan, query, key, value, keys_all, values_all, branch_low, w_out, attended, log_total, cosine, sine
    )
    d_key, d_value = owner(
        members, d_keys_all, d_values_all, d_key_own, d_value_own, cosine, sine
    )
    ffn, d_key = lax.optimization_barrier((ffn, d_key))
    own_out = (resid + ffn.astype(WIDE)).astype(LOW)
    layer_out = lax.all_gather(own_out, "tensor", axis=0, tiled=True).astype(WIDE)
    input_grad, grad_down, grad_out, grad_inner = first(
        count,
        members,
        d_query,
        d_key,
        d_value,
        w_query,
        w_key,
        w_value,
        grad_resid,
        states,
        act_one,
        mixed,
        branch_low,
        hidden,
        out_low,
    )
    width = d_query.shape[1]
    return (
        layer_out,
        input_grad.astype(WIDE),
        grad_inner[:, :width].astype(WIDE),
        grad_inner[:, width : 2 * width].astype(WIDE),
        grad_inner[:, 2 * width :].astype(WIDE),
        grad_out.astype(WIDE).T,
        grad_gate.astype(WIDE),
        grad_up.astype(WIDE),
        grad_down.astype(WIDE).T,
    )


def solution(mesh):
    placed = (
        P("dp", None),
        P(None, "tensor"),
        P(None, "tensor"),
        P(None, "tensor"),
        P("tensor", None),
        P(None, "tensor"),
        P(None, "tensor"),
        P("tensor", None),
        P(),
        P(),
        P("dp"),
        P("dp", None),
    )
    return jax.shard_map(
        body,
        mesh=mesh,
        in_specs=placed,
        out_specs=(
            P("dp", None),
            P("dp", None),
            P("dp", "tensor"),
            P("dp", "tensor"),
            P("dp", "tensor"),
            P("tensor", "dp"),
            P("dp", "tensor"),
            P("dp", "tensor"),
            P("tensor", "dp"),
        ),
        check_vma=False,
    )
```

time: 1280 us -> 507 us (0.40)
  waiting for transfers between devices: 926 us -> 0.06 us
  Pallas kernels: 0 us -> 455 us
  matrix products: 199 us -> 0 us
  other arithmetic: 74.8 us -> 21.3 us
  local copies, waits for them, and re-layouts: 56.2 us -> 5.32 us
    psum x3 -> x0, waiting for transfers between devices: 465 us -> none  [the longest x1 156 us: body(): lax.psum(jnp.dot(hidden, w_down, preferred_element_type=jnp.float32).asty...]
    pallas_call x0 -> x8, Pallas kernels: none -> 455 us  [the longest x1 119 us: first(): pl.pallas_call(functools.partial(first_kernel, count, pairs), out_shape=[...]
    reduce_scatter x7 -> x1, waiting for transfers between devices: 339 us -> 0.02 us  [body(): ffn = lax.psum_scatter(ffn, 'tensor', scatter_dimension=0, tiled=True)]
    dot_general x49 -> x0, matrix products: 199 us -> none  [the longest x34 142 us: contract(): lax.dot_general(left_side, right_side, (((left_dim,), (right_dim,)), ((),...]
    unnamed x16 -> x2, waiting for transfers between devices: 72.1 us -> 0.03 us
    all_gather x2 -> x1, waiting for transfers between devices: 49.7 us -> 0.01 us  [body(): lax.all_gather(own_out, 'tensor', axis=0, tiled=True).astype(WIDE)]
    unnamed x74 -> x12, local copies, waits for them, and re-layouts: 22.8 us -> 2.83 us
    reduce_sum x10 -> x1, other arithmetic: 20.1 us -> 0.87 us  [in_order(): return jnp.sum(jnp.where(found, everyone[None, :], 0), axis=1)]
  transfers between devices with their start and end apart: 14 -> 2, of which waited for: 13 -> 0; matrix products, arithmetic and copies ran while one was open for 8% -> 3% of each run, Pallas kernels for 0% -> 37%
where the time goes in v1:
time: 507 us; the launch traced here: 499 us
  Pallas kernels  455 us (90%)
  other arithmetic  21.3 us (4%)
  between operations  17.2 us (3%)
  local copies, waits for them, and re-layouts  5.32 us (1%)
    pallas_call x1, Pallas kernels, first(): pl.pallas_call(functools.partial(first_kernel, count, pairs), out_shape=[...  119 us
    pallas_call x1, Pallas kernels, second(): pl.pallas_call(functools.partial(second_kernel, count, pairs), out_shape=...  87.4 us
    pallas_call x1, Pallas kernels, branch(): pl.pallas_call(functools.partial(branch_kernel, count), out_shape=[shape(...  80.6 us
    pallas_call x1, Pallas kernels, project(): pl.pallas_call(functools.partial(project_kernel, members), out_shape=[sha...  44 us
    pallas_call x1, Pallas kernels, owner(): pl.pallas_call(functools.partial(owner_kernel, pairs), out_shape=[shape((...  39.4 us
    pallas_call x1, Pallas kernels, feed(): pl.pallas_call(feed_kernel, out_shape=[shape((rows, depth), LOW)] * 2 + [...  38.3 us
    pallas_call x1, Pallas kernels, attend_back(): pl.pallas_call(functools.partial(attend_back_kernel, members // 2), out_s...  28 us
    pallas_call x1, Pallas kernels, attend(): pl.pallas_call(functools.partial(attend_kernel, members // 2), out_shape=...  18.3 us
  transfers between devices with their start and end apart: 2, of which 0 were waited for; matrix products, arithmetic and copies ran while one was open for 3% of the time, Pallas kernels for 37%

profile of v1, /device:TPU:0, one launch (start us, length us, event | category | flops | bytes accessed | tf_op | source)
XLA Modules:
  0.0 499.3 jit_solution(383034813457463623)
XLA Ops:
  7.2 0.0 reduce-scatter.2.cloned.1.call-start
  7.2 1.2 dynamic_slice.7
  10.4 0.7 select_convert_fusion
  11.8 1.2 dynamic_slice.8
  13.0 1.3 broadcast_compare_fusion
  14.3 1.0 fusion
  15.3 0.9 select_reduce_fusion.1
  16.2 1.0 pad_maximum_fusion
  17.2 0.6 pad_add_fusion.plan
  17.8 44.0 %project.1 = (bf16[512,2048]{1,0:T(8,128)(2,1)}, bf16[512,512]{1,0:T(8,128)(2,1)}, bf16[512,512]{1,0:T(8,128)(2,1)}, bf16[512,512]{1,0:T(8,128)(2,1)}, bf16[512,...) custom-call(f32[512,2048]{1,0:T(8,128)} %states.5, bf16[2048,512]{1,0:T(8,128)(2,1)} %w_query.3, ...), custom_call_target="tpu_custom_call" | custom-call | tf_op jit(solution)/shard_map/project/pallas_call | solution.py:507
  61.7 18.3 %attend.1 = (bf16[512,512]{1,0:T(8,128)(2,1)}, f32[512,512]{1,0:T(8,128)}, f32[512,512]{1,0:T(8,128)}) custom-call(s32[10]{0:T(128)} %pad_add_fusion.plan, bf16[512,512]{1,0:T(8,128)(2,1)} %get-tuple-element.45.query, bf16[512,512]{1,0:T(8,128)(2,1)} %get-tuple-element.46.key, bf16[512,512]{1,0:T(8,128)(2,1)} %get-tuple-element.47.value, ...), custom_call_target="tpu_custom_call" | custom-call | tf_op jit(solution)/shard_map/attend/pallas_call | solution.py:569
  80.0 80.6 %branch.1 = (bf16[512,2048]{1,0:T(8,128)(2,1)}, f32[128,2048]{1,0:T(8,128)}) custom-call(bf16[512,512]{1,0:T(8,128)(2,1)} %get-tuple-element.50.mixed, bf16[512,2048]{1,0:T(8,128)(2,1)} %w_out.3, f32[512,2048]{1,0:T(8,128)} %states.5), custom_call_target="tpu_custom_call" | custom-call | tf_op jit(solution)/shard_map/branch/pallas_call | solution.py:733
  160.6 38.3 %feed.1 = (bf16[512,2048]{1,0:T(8,128)(2,1)}, bf16[512,2048]{1,0:T(8,128)(2,1)}, bf16[512,2048]{1,0:T(8,128)(2,1)}, bf16[512,2048]{1,0:T(8,128)(2,1)}, bf16[512,2048]{1,0:T(8,128)(2,1)}) custom-call(bf16[512,2048]{1,0:T(8,128)(2,1)} %get-tuple-element.52.act, bf16[512,2048]{1,0:T(8,128)(2,1)} %get-tuple-element.53.out_low, bf16[2048,2048]{1,0:T(8,128)(2,1)} %w_gate.1, ...), custom_call_target="tpu_custom_call" | custom-call | tf_op jit(solution)/shard_map/feed/pallas_call | solution.py:785
  198.9 87.4 %second.1 = (bf16[512,2048]{1,0:T(8,128)(2,1)}, f32[128,2048]{1,0:T(8,128)}, bf16[256,2048]{1,0:T(8,128)(2,1)}, bf16[256,2048]{1,0:T(8,128)(2,1)}) custom-call(bf16[512,2048]{1,0:T(8,128)(2,1)} %get-tuple-element.55.d_act, f32[128,2048]{1,0:T(8,128)} %get-tuple-element.51.resid, f32[512,2048]{1,0:T(8,128)} %cotangent.3, ...), custom_call_target="tpu_custom_call" | custom-call | tf_op jit(solution)/shard_map/second/pallas_call | solution.py:865
  286.4 0.0 reduce-scatter.2.cloned.1.call-update
  286.4 0.0 all-gather.2.cloned.1.call-start
  286.4 28.0 %attend_back.1 = (bf16[512,512]{1,0:T(8,128)(2,1)}, bf16[8,384,512]{2,1,0:T(8,128)(2,1)}, bf16[8,384,512]{2,1,0:T(8,128)(2,1)}, bf16[128,512]{1,0:T(8,128)(2,1)}, bf16[128,512]{1,0:T(8,128)(2,1)}) custom-call(s32[10]{0:T(128)} %pad_add_fusion.plan, bf16[512,512]{1,0:T(8,128)(2,1)} %get-tuple-element.45.query, bf16[512,512]{1,0:T(8,128)(2,1)} %get-tuple-element.46.key, ...), custom_call_target="tpu_custom_call" | custom-call | tf_op jit(solution)/shard_map/attend_back/pallas_call | solution.py:670
  314.5 0.0 copy-start
  314.5 39.4 %owner.1 = (bf16[512,512]{1,0:T(8,128)(2,1)}, bf16[512,512]{1,0:T(8,128)(2,1)}) custom-call(bf16[8,384,512]{2,1,0:T(8,128)(2,1)} %get-tuple-element.63.d_keys_all, bf16[8,384,512]{2,1,0:T(8,128)(2,1)} %get-tuple-element.64.d_values_all, bf16[128,512]{1,0:T(8,128)(2,1)} %get-tuple-element.65.d_key_own, bf16[128,512]{1,0:T(8,128)(2,1)} %get-tuple-element.66.d_value_own, ...), custom_call_target="tpu_custom_call" | custom-call | tf_op jit(solution)/shard_map/owner/pallas_call | solution.py:976
  353.9 0.0 copy-start.2
  353.9 0.0 reduce-scatter.2.cloned.1.call-done
  353.9 0.0 copy-done
  353.9 2.0 add_convert_fusion
  355.9 0.0 copy-start.1
  355.9 0.0 all-gather.2.cloned.1.call-update
  356.0 0.0 copy-done.2
  356.0 1.6 convert_element_type.44
  357.5 0.0 copy-done.1
  357.5 1.6 convert_element_type.45
  359.1 119.3 %first.1 = (bf16[512,2048]{1,0:T(8,128)(2,1)}, bf16[256,2048]{1,0:T(8,128)(2,1)}, bf16[256,512]{1,0:T(8,128)(2,1)}, bf16[256,1536]{1,0:T(8,128)(2,1)}) custom-call(bf16[512,512]{1,0:T(8,128)(2,1)} %get-tuple-element.69.d_query.far_query, bf16[512,512]{1,0:T(8,128)(2,1)} %get-tuple-element.70.d_key.far_key, ...), custom_call_target="tpu_custom_call" | custom-call | tf_op jit(solution)/shard_map/first/pallas_call | solution.py:1092
  478.4 1.0 convert_bitcast_fusion.1
  479.4 1.0 copy.23
  480.4 0.0 copy-start.3
  480.4 4.2 convert_element_type.40
  484.6 0.0 copy-done.3
  484.6 0.2 convert_bitcast_fusion
  484.9 0.0 copy-start.4
  484.9 1.8 copy.24
  486.7 0.0 copy-done.4
  486.7 1.2 slice_convert_fusion
  487.9 0.0 all-gather.2.cloned.1.call-done
  487.9 4.1 convert_element_type.39
  (2 shorter events, 0.0 us)
Async XLA Ops:
  7.2 346.7 %reduce-scatter.2.cloned.1.call-start = ((), (), s32[]{:S(2)}) async-start(), calls=%async_computation.1 | async-start | bytes 2621440 | tf_op jit(solution)/shard_map/reduce_scatter | solution.py:1187
  286.4 201.5 %all-gather.2.cloned.1.call-start = ((), (), s32[]{:S(2)}) async-start(), calls=%async_computation.2 | async-start | bytes 2621440 | tf_op jit(solution)/shard_map/all_gather | solution.py:1196
  314.5 39.4 %copy-start = (f32[128,2048]{1,0:T(8,128)S(1)}, f32[128,2048]{1,0:T(8,128)}, u32[]{:S(2)}) copy-start(f32[128,2048]{1,0:T(8,128)} %get-tuple-element.51.resid) | copy-start | bytes 3145732
  353.9 2.1 copy-start.2
  355.9 1.6 copy-start.1
  480.4 4.2 copy-start.3
  484.9 1.8 copy-start.4
Sparse Core Ops, SparseCore 0:
  286.5 44.5 reduce-scatter.1
  356.1 73.7 all-gather.1
